TPU v7x, 32 devices: a whole 2x2x4 slice. The times are simulated.
32 devices in a mesh: groups: 2 (over x), blk: 16 (over z, y, core).
Axes of the slice: x: 2, y: 2, z: 4, core: 2. Of those that a mesh axis runs over, the one named last changes fastest.
Arguments:
- embeddings: bfloat16 [12288, 512], P(('groups', 'blk')), parts along dimension 0, may hold values from -24 to 24
- cluster_ids: int32 [12288], P(('groups', 'blk')), parts along dimension 0, may hold values from 0 to 63, as said below
- cluster_sizes: int32 [128], P('groups'), parts along dimension 0, may hold values from 12 to 960, as said below
Outputs:
- log_density: float32 [12288], P(('groups', 'blk')), parts along dimension 0
- centrality: float32 [12288], P(('groups', 'blk')), parts along dimension 0
There are 2 independent parts, one for each index of `groups`. A program takes and returns all parts, laid end to end along the dimension named above; each array names one. Nothing has to cross between parts.
Inputs may be any that keep to these rules, and one draw needn't show every extreme that they name: cluster_sizes[c] is the number of rows whose cluster id is c; the sizes sum to 6144 and the largest is exactly 960. `cluster_ids`: rows are dealt to the devices of blk: with n the number of devices of blk and E_c the sum of cluster_sizes[c'] mod n over the clusters c' < c, device s holds cluster_sizes[c] // n rows of cluster c, plus one more exactly when (s - E_c) mod n < cluster_sizes[c] mod n. Within a device the rows stand in no particular order.
All inputs are finite; a program needn't handle non-finite values.
Results may differ from a plain program's by a relative error of at most 0.00065.
The roundings to bfloat16 on the way count: a program that leaves them out, or rounds other values in their place, can miss the bound.
Values may be sent and summed in bfloat16 or wider, within the bound.
A program may use at most 64 MiB of HBM per device.

v0:
```python
import jax
import jax.numpy as jnp
from jax import lax
from jax.sharding import PartitionSpec as P

SOFTMAX_TEMP = 0.1
EPSILON = 1e-06


def shifted(array, axis, by):
    peers = lax.axis_size(axis)
    pairs = [(i, i + by) for i in range(peers) if 0 <= i + by < peers]
    return lax.ppermute(array, axis, pairs)


def unit_rows(embeddings):
    values = embeddings.astype(jnp.float32)
    scale = lax.rsqrt(jnp.mean(values * values, axis=1, keepdims=True) + EPSILON)
    return (values * (scale * values.shape[1] ** (-0.5))).astype(jnp.bfloat16)


def block_terms(remaining_rows, left_labels, right_rows, right_labels):
    similarity_scores = jnp.einsum(
        "rd,kd->rk", remaining_rows, right_rows, preferred_element_type=jnp.float32
    )
    same_cluster = left_labels[:, None] == right_labels[None, :]
    return jnp.sum(jnp.where(same_cluster, jnp.exp(similarity_scores / SOFTMAX_TEMP), 0.0), axis=1)


def lookup(table, one_hot):
    return jnp.sum(jnp.where(one_hot, table[None, :], 0), axis=1)


def sorted_density(unit, cluster_sizes, member):
    devices = lax.axis_size("blk")
    own_index = lax.axis_index("blk")
    rows_dev = unit.shape[0]
    clusters = cluster_sizes.shape[0]
    total_rows = rows_dev * devices
    fewest = total_rows // 512
    largest = total_rows * 5 // 32
    capacity = min(rows_dev, rows_dev // devices + rows_dev // fewest + 2)
    reach = (largest + rows_dev - 2) // rows_dev
    ends = jnp.cumsum(cluster_sizes)
    starts = ends - cluster_sizes
    base = cluster_sizes // devices
    extra = cluster_sizes % devices
    first = (jnp.cumsum(extra) - extra) % devices
    source_rows = jnp.arange(devices, dtype=jnp.int32)
    holds = base[None, :] + (
        (source_rows[:, None] - first[None, :]) % devices < extra[None, :]
    ).astype(jnp.int32)
    member_count = jnp.cumsum(member.astype(jnp.int32), axis=0)
    rank = jnp.sum(jnp.where(member, member_count - 1, 0), axis=1)
    held_row = jnp.dot(
        member.astype(jnp.float32), holds.T.astype(jnp.float32), precision=lax.Precision.HIGHEST
    ).astype(jnp.int32)
    before_me = (source_rows[None, :] < own_index) & (held_row > rank[:, None])
    within = jnp.sum(jnp.minimum(held_row, rank[:, None]), axis=1) + jnp.sum(
        before_me.astype(jnp.int32), axis=1
    )
    position = lookup(starts, member) + within
    target = position // rows_dev
    earlier = (target[None, :] == target[:, None]) & (position[None, :] < position[:, None])
    slot = jnp.sum(earlier.astype(jnp.int32), axis=1)
    address = target * capacity + slot
    sender = (
        jnp.zeros((devices * capacity,), jnp.int32)
        .at[address]
        .set(jnp.arange(rows_dev, dtype=jnp.int32))
    )
    filled = jnp.zeros((devices * capacity,), jnp.bool_).at[address].set(True)
    packed = jnp.where(filled[:, None], unit[sender], jnp.zeros((), jnp.bfloat16))
    arrived = lax.all_to_all(packed, "blk", split_axis=0, concat_axis=0, tiled=True)
    local = jnp.arange(rows_dev, dtype=jnp.int32)
    places = own_index * rows_dev + local
    home_label = jnp.sum((places[:, None] >= ends[None, :]).astype(jnp.int32), axis=1)
    home_cluster_member = home_label[:, None] == jnp.arange(clusters, dtype=jnp.int32)[None, :]
    offset_in = places - lookup(starts, home_cluster_member)
    base_row = lookup(base, home_cluster_member)
    extra_row = lookup(extra, home_cluster_member)
    first_row = lookup(first, home_cluster_member)
    full_rounds = devices * base_row
    surplus = offset_in - full_rounds
    wrapped = first_row + extra_row - devices
    late_source = jnp.where(
        wrapped > 0,
        jnp.where(surplus < wrapped, surplus, first_row + surplus - wrapped),
        first_row + surplus,
    )
    anchor = jnp.where(offset_in < full_rounds, offset_in % devices, late_source)
    anchor_hot = anchor[:, None] == source_rows[None, :]
    anchor_count = jnp.cumsum(anchor_hot.astype(jnp.int32), axis=0)
    order_in = jnp.sum(jnp.where(anchor_hot, anchor_count - 1, 0), axis=1)
    block = arrived[anchor * capacity + order_in]

    def labels_at(spots):
        inside = (spots >= 0) & (spots < total_rows)
        found = jnp.sum((spots[:, None] >= ends[None, :]).astype(jnp.int32), axis=1)
        return jnp.where(inside, found, -1)

    density = block_terms(block, home_label, block, home_label)

    def advance(offset, carried_rows):
        upper, lower, running = carried_rows
        upper = shifted(upper, "blk", 1)
        lower = shifted(lower, "blk", -1)
        running = running + block_terms(
            block, home_label, upper, labels_at(places - offset * rows_dev)
        )
        running = running + block_terms(
            block, home_label, lower, labels_at(places + offset * rows_dev)
        )
        return (upper, lower, running)

    carried_out = lax.fori_loop(1, reach + 1, advance, (block, block, density))
    density = carried_out[2]
    returned = (
        jnp.zeros((devices * capacity,), jnp.float32).at[anchor * capacity + order_in].set(density)
    )
    answered = lax.all_to_all(returned, "blk", split_axis=0, concat_axis=0, tiled=True)
    return answered[address]


def on_device(embeddings, cluster_ids, cluster_sizes):
    unit = unit_rows(embeddings)
    clusters = cluster_sizes.shape[0]
    member = cluster_ids[:, None] == jnp.arange(clusters, dtype=jnp.int32)[None, :]
    partial_sum = jnp.einsum(
        "rc,rd->cd", member.astype(jnp.bfloat16), unit, preferred_element_type=jnp.float32
    )
    centroid = lax.psum(partial_sum, "blk")
    density = sorted_density(unit, cluster_sizes, member)
    sizes_row = lookup(cluster_sizes, member).astype(jnp.float32)
    log_density = jnp.log(density / sizes_row)
    projected = jnp.dot(unit.astype(jnp.float32), centroid.T, precision=lax.Precision.HIGHEST)
    centrality = jnp.sum(jnp.where(member, projected, 0.0), axis=1) / sizes_row
    return (log_density, centrality)


def solution(mesh):
    in_specs = (P(("groups", "blk"), None), P(("groups", "blk")), P("groups"))
    out_specs = (P(("groups", "blk")), P(("groups", "blk")))
    return jax.shard_map(
        on_device, mesh=mesh, in_specs=in_specs, out_specs=out_specs, check_vma=False
    )
```

profile of v0, /device:TPU:0, one launch (start us, length us, event | category | flops | bytes accessed | tf_op | source)
XLA Modules:
  0.0 140.2 jit_solution(12733876175211087510)
XLA Ops:
  7.2 1.2 fusion.14
  8.6 0.6 copy-done.2
  10.0 0.6 copy-done.1
  10.6 0.9 reduce-window.41
  12.6 2.9 %scatter_custom_fusion.1 = s32[928]{0:T(1024)S(1)} fusion(s32[384]{0:T(512)S(1)} %fusion.58, s32[384]{0:T(512)S(1)} %iota.57, s32[]{:T(128)} %copy.40), kind=kCustom, calls=%fused_computation.120 | custom fusion | bytes 3716 | tf_op jit(solution)/shard_map/scatter | solution.py:70
  15.5 4.0 %gather_fusion = bf16[928,512]{1,0:T(8,128)(2,1)S(1)} fusion(bf16[384,512]{1,0:T(8,128)(2,1)S(1)} %fusion.15, s32[1024]{0:T(1024)S(1)} %pad_clamp_fusion.2), kind=kCustom, calls=%fused_computation | custom fusion | bytes 1904256 | tf_op jit(solution)/shard_map/gather | solution.py:73
  19.8 2.0 %scatter_custom_fusion = pred[928]{0:T(1024)(128)(4,1)S(1)} fusion(s32[384]{0:T(512)S(1)} %fusion.58, pred[384]{0:T(512)(128)(4,1)S(1)} %broadcast.470, pred[]{:T(512)} %constant.152.clone.1), kind=kCustom, calls=%fused_computation.132 | custom fusion | bytes 929 | tf_op jit(solution)/shard_map/scatter | solution.py:72
  21.9 1.2 broadcast_select_fusion
  23.1 7.4 %all-to-all-start = ((bf16[16,58,512]{2,1,0:T(8,128)(2,1)}), bf16[16,58,512]{2,1,0:T(8,128)(2,1)S(1)}, u32[]{:S(2)}, u32[]{:S(2)}) async-start(bf16[16,58,512]{2,1,0:T(8,128)(2,1)} %broadcast_select_fusion), calls=%async_computation | async-start | bytes 2097152 | tf_op jit(solution)/shard_map/all_to_all | solution.py:74
  30.6 0.8 fusion.18
  31.5 0.9 reduce-window.39
  32.8 21.2 %all-to-all-done = bf16[16,58,512]{2,1,0:T(8,128)(2,1)S(1)} async-done(((bf16[16,58,512]{2,1,0:T(8,128)(2,1)}), bf16[16,58,512]{2,1,0:T(8,128)(2,1)S(1)}, u32[]{:S(2)}, u32[]{:S(2)}) %all-to-all-start) | async-done | bytes 950304 | tf_op jit(solution)/shard_map/all_to_all | solution.py:74
  54.3 2.1 %gather_fusion.1 = bf16[384,512]{1,0:T(8,128)(2,1)S(1)} fusion(bf16[928,512]{1,0:T(8,128)(2,1)S(1)} %all_to_all.15, s32[1024]{0:T(1024)S(1)} %pad_clamp_fusion.1), kind=kCustom, calls=%fused_computation.1 | custom fusion | bytes 787968 | tf_op jit(solution)/shard_map/gather | solution.py:95
  56.8 34.6 %while.18 = (s32[]{:T(128)}, bf16[384,512]{1,0:T(8,128)(2,1)S(1)}, bf16[384,512]{1,0:T(8,128)(2,1)S(1)}, f32[384]{0:T(512)S(1)}, s32[384]{0:T(512)S(1)}, /*index...) while((s32[]{:T(128)}, bf16[384,512]{1,0:T(8,128)(2,1)S(1)}, ...), condition=%wide.region_26.27_spmd.clone, body=%wide.region_21.26_spmd.clone.sunk | while | flops 303321984 | bytes 6322649 | solution.py:116
  56.8 2.5 %collective-permute-start = (bf16[384,512]{1,0:T(8,128)(2,1)S(1)}, bf16[384,512]{1,0:T(8,128)(2,1)S(1)}, u32[]{:S(2)}, u32[]{:S(2)}) collective-permute-start(bf16[384,512]{1,0:T(8,128)(2,1)S(1)} %get-tuple-element.275), channel_id=1, source_target_pairs={{0,1},{1,2},{2,3},{3,4},{4,5},{5,6},{6,7},{7,8},{8,9},{9,10},{10,1... | collective-permute-start | bytes 1179656 | tf_op jit(solution)/shard_map/while/body/eval_jaxpr/ppermute | solution.py:13
  59.3 1.3 collective-permute-start.1
  60.8 3.0 %collective-permute-done.1 = bf16[384,512]{1,0:T(8,128)(2,1)S(1)} collective-permute-done((bf16[384,512]{1,0:T(8,128)(2,1)S(1)}, bf16[384,512]{1,0:T(8,128)(2,1)S(1)}, u32[]{:S(2)}, u32[]{:S(2)}) %collective-permute-start.1) | collective-permute-done | bytes 393248 | tf_op jit(solution)/shard_map/while/body/eval_jaxpr/ppermute | solution.py:13
  64.7 7.9 %collective-permute-start = (bf16[384,512]{1,0:T(8,128)(2,1)S(1)}, bf16[384,512]{1,0:T(8,128)(2,1)S(1)}, u32[]{:S(2)}, u32[]{:S(2)}) collective-permute-start(bf16[384,512]{1,0:T(8,128)(2,1)S(1)} %get-tuple-element.275), channel_id=1, source_target_pairs={{0,1},{1,2},{2,3},{3,4},{4,5},{5,6},{6,7},{7,8},{8,9},{9,10},{10,1... | collective-permute-start | bytes 1179656 | tf_op jit(solution)/shard_map/while/body/eval_jaxpr/ppermute | solution.py:13
  72.6 1.3 collective-permute-start.1
  74.1 2.2 %collective-permute-done.1 = bf16[384,512]{1,0:T(8,128)(2,1)S(1)} collective-permute-done((bf16[384,512]{1,0:T(8,128)(2,1)S(1)}, bf16[384,512]{1,0:T(8,128)(2,1)S(1)}, u32[]{:S(2)}, u32[]{:S(2)}) %collective-permute-start.1) | collective-permute-done | bytes 393248 | tf_op jit(solution)/shard_map/while/body/eval_jaxpr/ppermute | solution.py:13
  77.2 9.6 %collective-permute-start = (bf16[384,512]{1,0:T(8,128)(2,1)S(1)}, bf16[384,512]{1,0:T(8,128)(2,1)S(1)}, u32[]{:S(2)}, u32[]{:S(2)}) collective-permute-start(bf16[384,512]{1,0:T(8,128)(2,1)S(1)} %get-tuple-element.275), channel_id=1, source_target_pairs={{0,1},{1,2},{2,3},{3,4},{4,5},{5,6},{6,7},{7,8},{8,9},{9,10},{10,1... | collective-permute-start | bytes 1179656 | tf_op jit(solution)/shard_map/while/body/eval_jaxpr/ppermute | solution.py:13
  86.9 1.3 collective-permute-start.1
  88.3 2.2 %collective-permute-done.1 = bf16[384,512]{1,0:T(8,128)(2,1)S(1)} collective-permute-done((bf16[384,512]{1,0:T(8,128)(2,1)S(1)}, bf16[384,512]{1,0:T(8,128)(2,1)S(1)}, u32[]{:S(2)}, u32[]{:S(2)}) %collective-permute-start.1) | collective-permute-done | bytes 393248 | tf_op jit(solution)/shard_map/while/body/eval_jaxpr/ppermute | solution.py:13
  91.4 2.9 %scatter_custom_fusion.2 = f32[928]{0:T(1024)S(1)} fusion(s32[384]{0:T(512)S(1)} %fusion.57, f32[384]{0:T(512)S(1)} %get-tuple-element.141, f32[]{:T(128)} %constant.139.clone.1), kind=kCustom, calls=%fused_computation.128 | custom fusion | bytes 3716 | tf_op jit(solution)/shard_map/scatter | solution.py:119
  94.3 0.7 all_to_all.16
  95.0 14.0 %all-to-all-start.1 = ((f32[16,58,1]{1,2,0:T(1,128)}), f32[16,58,1]{1,2,0:T(1,128)S(1)}, u32[]{:S(2)}, u32[]{:S(2)}) async-start(f32[16,58,1]{1,2,0:T(1,128)} %bitcast.9), calls=%async_computation.1 | async-start | bytes 16384 | tf_op jit(solution)/shard_map/all_to_all | solution.py:121
  109.0 19.2 %all-reduce.2.cloned.1.call-done = f32[64,512]{1,0:T(8,128)} async-done(((f32[64,512]{1,0:T(8,128)}), f32[64,512]{1,0:T(8,128)}) %all-reduce.2.cloned.1.call-update) | async-done | bytes 131088 | tf_op jit(solution)/shard_map/psum | solution.py:132
  128.1 1.4 fusion.13
  129.5 0.5 broadcast.549
  130.1 0.7 reduce.13
  130.8 1.9 %gather_fusion.2 = f32[384]{0:T(512)S(1)} fusion(f32[928]{0:T(1024)S(1)} %all_to_all.18, s32[1024]{0:T(1024)S(1)} %pad_clamp_fusion), kind=kCustom, calls=%fused_computation.2 | custom fusion | bytes 4608 | tf_op jit(solution)/shard_map/gather | solution.py:122
  132.7 0.6 convert_divide_fusion
  (78 shorter events, 6.6 us)
Async XLA Ops:
  7.2 1.2 copy-start
  8.6 0.7 copy-start.2
  9.9 0.7 copy-start.1
  23.1 30.9 %all-to-all-start = ((bf16[16,58,512]{2,1,0:T(8,128)(2,1)}), bf16[16,58,512]{2,1,0:T(8,128)(2,1)S(1)}, u32[]{:S(2)}, u32[]{:S(2)}) async-start(bf16[16,58,512]{2,1,0:T(8,128)(2,1)} %broadcast_select_fusion), calls=%async_computation | async-start | bytes 2097152 | tf_op jit(solution)/shard_map/all_to_all | solution.py:74
  30.5 97.6 %all-reduce.2.cloned.1.call-start = ((), (), s32[]{:S(2)}) async-start(), calls=%async_computation.2 | async-start | bytes 262144 | tf_op jit(solution)/shard_map/psum | solution.py:132
  56.8 7.4 %collective-permute-start = (bf16[384,512]{1,0:T(8,128)(2,1)S(1)}, bf16[384,512]{1,0:T(8,128)(2,1)S(1)}, u32[]{:S(2)}, u32[]{:S(2)}) collective-permute-start(bf16[384,512]{1,0:T(8,128)(2,1)S(1)} %get-tuple-element.275), channel_id=1, source_target_pairs={{0,1},{1,2},{2,3},{3,4},{4,5},{5,6},{6,7},{7,8},{8,9},{9,10},{10,1... | collective-permute-start | bytes 1179656 | tf_op jit(solution)/shard_map/while/body/eval_jaxpr/ppermute | solution.py:13
  59.3 4.5 %collective-permute-start.1 = (bf16[384,512]{1,0:T(8,128)(2,1)S(1)}, bf16[384,512]{1,0:T(8,128)(2,1)S(1)}, u32[]{:S(2)}, u32[]{:S(2)}) collective-permute-start(bf16[384,512]{1,0:T(8,128)(2,1)S(1)} %get-tuple-element.276), channel_id=1, source_target_pairs={{1,0},{2,1},{3,2},{4,3},{5,4},{6,5},{7,6},{8,7},{9,8},{10,9},{11,1... | collective-permute-start | bytes 1179656 | tf_op jit(solution)/shard_map/while/body/eval_jaxpr/ppermute | solution.py:13
  64.7 12.0 %collective-permute-start = (bf16[384,512]{1,0:T(8,128)(2,1)S(1)}, bf16[384,512]{1,0:T(8,128)(2,1)S(1)}, u32[]{:S(2)}, u32[]{:S(2)}) collective-permute-start(bf16[384,512]{1,0:T(8,128)(2,1)S(1)} %get-tuple-element.275), channel_id=1, source_target_pairs={{0,1},{1,2},{2,3},{3,4},{4,5},{5,6},{6,7},{7,8},{8,9},{9,10},{10,1... | collective-permute-start | bytes 1179656 | tf_op jit(solution)/shard_map/while/body/eval_jaxpr/ppermute | solution.py:13
  72.6 3.6 %collective-permute-start.1 = (bf16[384,512]{1,0:T(8,128)(2,1)S(1)}, bf16[384,512]{1,0:T(8,128)(2,1)S(1)}, u32[]{:S(2)}, u32[]{:S(2)}) collective-permute-start(bf16[384,512]{1,0:T(8,128)(2,1)S(1)} %get-tuple-element.276), channel_id=1, source_target_pairs={{1,0},{2,1},{3,2},{4,3},{5,4},{6,5},{7,6},{8,7},{9,8},{10,9},{11,1... | collective-permute-start | bytes 1179656 | tf_op jit(solution)/shard_map/while/body/eval_jaxpr/ppermute | solution.py:13
  77.2 13.7 %collective-permute-start = (bf16[384,512]{1,0:T(8,128)(2,1)S(1)}, bf16[384,512]{1,0:T(8,128)(2,1)S(1)}, u32[]{:S(2)}, u32[]{:S(2)}) collective-permute-start(bf16[384,512]{1,0:T(8,128)(2,1)S(1)} %get-tuple-element.275), channel_id=1, source_target_pairs={{0,1},{1,2},{2,3},{3,4},{4,5},{5,6},{6,7},{7,8},{8,9},{9,10},{10,1... | collective-permute-start | bytes 1179656 | tf_op jit(solution)/shard_map/while/body/eval_jaxpr/ppermute | solution.py:13
  86.9 3.6 %collective-permute-start.1 = (bf16[384,512]{1,0:T(8,128)(2,1)S(1)}, bf16[384,512]{1,0:T(8,128)(2,1)S(1)}, u32[]{:S(2)}, u32[]{:S(2)}) collective-permute-start(bf16[384,512]{1,0:T(8,128)(2,1)S(1)} %get-tuple-element.276), channel_id=1, source_target_pairs={{1,0},{2,1},{3,2},{4,3},{5,4},{6,5},{7,6},{8,7},{9,8},{10,9},{11,1... | collective-permute-start | bytes 1179656 | tf_op jit(solution)/shard_map/while/body/eval_jaxpr/ppermute | solution.py:13
  95.0 34.5 %all-to-all-start.1 = ((f32[16,58,1]{1,2,0:T(1,128)}), f32[16,58,1]{1,2,0:T(1,128)S(1)}, u32[]{:S(2)}, u32[]{:S(2)}) async-start(f32[16,58,1]{1,2,0:T(1,128)} %bitcast.9), calls=%async_computation.1 | async-start | bytes 16384 | tf_op jit(solution)/shard_map/all_to_all | solution.py:121
Sparse Core Ops, SparseCore 0:
  34.8 93.2 all-reduce.1
where the time goes:
time: 142 us; the launch traced here: 140 us
  waiting for transfers between devices  47.8 us (34%)
  starting transfers between devices  45.3 us (32%)
  local copies, waits for them, and re-layouts  19.8 us (14%)
  between operations  14.3 us (10%)
  other arithmetic  7.29 us (5%)
  matrix products  5.41 us (4%)
    ppermute x6, starting transfers between devices, shifted(): return lax.ppermute(array, axis, pairs)  23.9 us
    all_to_all x1, waiting for transfers between devices, sorted_density(): lax.all_to_all(packed, 'blk', split_axis=0, concat_axis=0, tiled=True)  21.2 us
    psum x1, waiting for transfers between devices, on_device(): centroid = lax.psum(partial_sum, 'blk')  19.2 us
    all_to_all x1, starting transfers between devices, sorted_density(): lax.all_to_all(returned, 'blk', split_axis=0, concat_axis=0, tiled=True)  14 us
    ppermute x6, waiting for transfers between devices, shifted(): return lax.ppermute(array, axis, pairs)  7.4 us
    all_to_all x1, starting transfers between devices, sorted_density(): lax.all_to_all(packed, 'blk', split_axis=0, concat_axis=0, tiled=True)  7.39 us
    gather x2, local copies, waits for them, and re-layouts, sorted_density(): unit[sender]  4.29 us
    scatter x1, local copies, waits for them, and re-layouts, sorted_density(): jnp.zeros((devices * capacity,), jnp.float32)  2.92 us
  transfers between devices with their start and end apart: 9, of which 5 were waited for; matrix products, arithmetic and copies ran while one was open for 9% of the time, Pallas kernels for 0%

commit v1 on v0

v1 whole, which is shorter than its diff:
```python
import functools

import jax
import jax.numpy as jnp
from jax import lax
from jax.experimental import pallas as pl
from jax.experimental.pallas import tpu as pltpu
from jax.sharding import PartitionSpec as P

SOFTMAX_TEMP = 0.1
EPSILON = 1e-06
LANES = 128
MESH = pl.DeviceIdType.MESH
F32 = jnp.float32
BF16 = jnp.bfloat16
NT = (((1,), (1,)), ((), ()))


def iota(shape, dim):
    return lax.broadcasted_iota(jnp.int32, shape, dim)


def loop(count, body):
    if count <= 8:
        for step in range(count):
            body(step)
    else:
        lax.fori_loop(0, count, lambda step, carry: (body(step), carry)[1], 0)


def kernel(n, cap, limit, emb_ref, ids_ref, sizes_ref, dens_ref, cent_ref,
           packed, packed_lab, own, other, own_lab, other_lab, ret, ret_in, addr_ref,
           send, recv, send_lab, recv_lab, fsend, frecv, fsend_lab, frecv_lab, rsend, rrecv):
    bins = n // 2
    rows, width = emb_ref.shape
    clusters = sizes_ref.shape[1]
    me = lax.axis_index("blk")
    chip = lax.div(me, 2)
    core = lax.rem(me, 2)
    partner = 2 * chip + 1 - core

    def peer(step):
        return 2 * lax.rem(chip + step, bins) + core

    def back(step):
        return 2 * lax.rem(chip + bins - step, bins) + core

    barrier = pltpu.get_barrier_semaphore()
    pl.semaphore_signal(barrier, inc=1, device_id={"blk": partner}, device_id_type=MESH)
    loop(bins - 1, lambda s: pl.semaphore_signal(
        barrier, inc=1, device_id={"blk": peer(s + 1)}, device_id_type=MESH))

    values = emb_ref[...].astype(F32)
    scale = lax.rsqrt(jnp.mean(values * values, axis=1, keepdims=True) + EPSILON)
    unit = (values * (scale * width ** (-0.5))).astype(BF16)

    sizes_row = sizes_ref[...].astype(F32)
    above = iota((clusters, clusters), 0)
    along = iota((clusters, clusters), 1)
    ends = jnp.sum(jnp.where(along <= above, sizes_row, 0.0), axis=1, keepdims=True)
    sizes = jnp.sum(jnp.where(along == above, sizes_row, 0.0), axis=1, keepdims=True)
    starts = ends - sizes
    edge = jnp.zeros((1, 1), F32)
    bin_of = jnp.zeros((clusters, 1), F32)
    for _ in range(bins - 1):
        edge = jnp.max(jnp.where(ends <= edge + limit, ends, 0.0), axis=0, keepdims=True)
        bin_of += jnp.where(starts >= edge, 1.0, 0.0)

    ids = ids_ref[...]
    member = iota((clusters, rows), 0) == ids
    bin_row = jnp.sum(jnp.where(member, bin_of, 0.0), axis=0, keepdims=True)
    size_row = jnp.sum(jnp.where(member, sizes, 0.0), axis=0, keepdims=True)
    shown = max(bins, 8)
    in_bin = iota((shown, rows), 0).astype(F32) == bin_row
    before = jnp.where(iota((rows, rows), 0) < iota((rows, rows), 1), 1.0, 0.0).astype(BF16)
    rank = jnp.dot(jnp.where(in_bin, 1.0, 0.0).astype(BF16), before, preferred_element_type=F32)
    slot = jnp.sum(jnp.where(in_bin, rank, 0.0), axis=0, keepdims=True)
    address = (bin_row * LANES + slot).astype(jnp.int32)
    addr_ref[...] = jnp.broadcast_to(address, addr_ref.shape)
    label_rows = jnp.broadcast_to((ids + 1).astype(F32), (8, rows)).astype(BF16)

    def hot(step):
        place = lax.rem(chip + step, bins) * LANES
        return iota((LANES, rows), 0) + place == addr_ref[0:1, :]

    def data_copy(step):
        return pltpu.make_async_remote_copy(
            packed.at[step, pl.ds(0, cap)], own.at[step, pl.ds(0, cap)],
            send.at[step], recv.at[step], device_id={"blk": peer(step)}, device_id_type=MESH)

    def label_copy(step):
        return pltpu.make_async_remote_copy(
            packed_lab.at[step], own_lab.at[step], send_lab.at[step], recv_lab.at[step],
            device_id={"blk": peer(step)}, device_id_type=MESH)

    def forward_copy(step):
        return pltpu.make_async_remote_copy(
            own.at[step, pl.ds(0, cap)], other.at[step, pl.ds(0, cap)],
            fsend.at[step], frecv.at[step], device_id={"blk": partner}, device_id_type=MESH)

    def forward_label_copy(step):
        return pltpu.make_async_remote_copy(
            own_lab.at[step], other_lab.at[step], fsend_lab.at[step], frecv_lab.at[step],
            device_id={"blk": partner}, device_id_type=MESH)

    def return_copy(step):
        return pltpu.make_async_remote_copy(
            ret.at[step], ret_in.at[step], rsend.at[step], rrecv.at[step],
            device_id={"blk": back(step)}, device_id_type=MESH)

    def pack(step, rows_ref, lab_ref):
        one_hot = jnp.where(hot(step), 1.0, 0.0).astype(BF16)
        rows_ref[step] = jnp.dot(one_hot, unit, preferred_element_type=F32).astype(BF16)
        lab_ref[step] = lax.dot_general(label_rows, one_hot, NT, preferred_element_type=F32)

    pl.semaphore_wait(barrier, bins)

    def send_step(s):
        pack(s + 1, packed, packed_lab)
        data_copy(s + 1).start()
        label_copy(s + 1).start()

    loop(bins - 1, send_step)
    pack(0, own, own_lab)
    forward_copy(0).start()
    forward_label_copy(0).start()
    if cap < LANES:
        def clear(s):
            own[s + 1, cap:, :] = jnp.zeros((LANES - cap, width), BF16)
        loop(bins - 1, clear)

    def pass_on(s):
        data_copy(s + 1).wait_recv()
        forward_copy(s + 1).start()
        label_copy(s + 1).wait_recv()
        forward_label_copy(s + 1).start()

    loop(bins - 1, pass_on)

    def arrived(s):
        forward_copy(s).wait_recv()
        forward_label_copy(s).wait_recv()

    loop(bins, arrived)

    def scores(side, lab, pair, total):
        left = side[:, :cap, :].reshape(bins * cap, width)
        columns = lab[:, 0, :].T
        left_lab = jnp.concatenate([columns[:cap, s:s + 1] for s in range(bins)], axis=0)
        right = own[pl.ds(2 * pair, 2)].reshape(2 * LANES, width)
        right_lab = jnp.concatenate(
            [own_lab[2 * pair, 0:1, :], own_lab[2 * pair + 1, 0:1, :]], axis=1)
        cosine = lax.dot_general(left, right, NT, preferred_element_type=F32)
        same = left_lab == right_lab
        dens = jnp.sum(jnp.where(same, jnp.exp(cosine * (1.0 / SOFTMAX_TEMP)), 0.0),
                       axis=0, keepdims=True)
        cent = jnp.sum(jnp.where(same, cosine, 0.0), axis=0, keepdims=True)
        return total[0] + dens, total[1] + cent

    def work(pair):
        none = jnp.zeros((1, 2 * LANES), F32)
        total = scores(own, own_lab, pair, (none, none))
        dens, cent = scores(other, other_lab, pair, total)
        for half in range(2):
            part = slice(half * LANES, (half + 1) * LANES)
            ret[2 * pair + half] = jnp.concatenate(
                [dens[:, part], cent[:, part], jnp.zeros((6, LANES), F32)], axis=0)

    lax.fori_loop(0, bins // 2, lambda pair, carry: (work(pair), carry)[1], 0)
    loop(bins - 1, lambda s: return_copy(s + 1).start())
    ret_in[0] = ret[0]
    loop(bins - 1, lambda s: return_copy(s + 1).wait_recv())

    def gathered(step, total):
        answer = ret_in[step].T
        mine = hot(step)
        return (total[0] + jnp.where(mine, answer[:, 0:1], 0.0),
                total[1] + jnp.where(mine, answer[:, 1:2], 0.0))

    none = jnp.zeros((LANES, rows), F32)
    dens, cent = lax.fori_loop(0, bins, gathered, (none, none))
    dens_ref[...] = jnp.log(jnp.sum(dens, axis=0, keepdims=True) / size_row)
    cent_ref[...] = jnp.sum(cent, axis=0, keepdims=True) / size_row

    def finish(s):
        data_copy(s + 1).wait_send()
        label_copy(s + 1).wait_send()
        return_copy(s + 1).wait_send()

    loop(bins - 1, finish)

    def finish_forward(s):
        forward_copy(s).wait_send()
        forward_label_copy(s).wait_send()

    loop(bins, finish_forward)


def on_device(embeddings, cluster_ids, cluster_sizes):
    n = lax.axis_size("blk")
    rows, width = embeddings.shape
    bins = n // 2
    total = rows * n
    limit = max(2 * total // bins, total * 5 // 32)
    cap = -(-(-(-limit // n)) // 16) * 16
    vmem = pl.BlockSpec(memory_space=pltpu.VMEM)
    dma = pltpu.SemaphoreType.DMA((bins,))
    dens, cent = pl.pallas_call(
        functools.partial(kernel, n, cap, float(limit)),
        out_shape=[jax.ShapeDtypeStruct((1, rows), F32)] * 2,
        in_specs=[vmem] * 3,
        out_specs=[vmem] * 2,
        scratch_shapes=[
            pltpu.VMEM((bins, LANES, width), BF16),
            pltpu.VMEM((bins, 8, LANES), F32),
            pltpu.VMEM((bins, LANES, width), BF16),
            pltpu.VMEM((bins, LANES, width), BF16),
            pltpu.VMEM((bins, 8, LANES), F32),
            pltpu.VMEM((bins, 8, LANES), F32),
            pltpu.VMEM((bins, 8, LANES), F32),
            pltpu.VMEM((bins, 8, LANES), F32),
            pltpu.VMEM((8, rows), jnp.int32),
        ] + [dma] * 10,
        compiler_params=pltpu.CompilerParams(
            collective_id=0, has_side_effects=True, vmem_limit_bytes=48 * 1024 * 1024),
        cost_estimate=pl.CostEstimate(flops=4 * 10 ** 9, bytes_accessed=10 ** 6, transcendentals=0),
    )(embeddings, cluster_ids[None, :], cluster_sizes[None, :])
    return dens[0], cent[0]


def solution(mesh):
    in_specs = (P(("groups", "blk"), None), P(("groups", "blk")), P("groups"))
    out_specs = (P(("groups", "blk")), P(("groups", "blk")))
    return jax.shard_map(
        on_device, mesh=mesh, in_specs=in_specs, out_specs=out_specs, check_vma=False
    )
```

time: 142 us -> 40.4 us (0.28); the launches traced: 140 us -> 40 us
  waiting for transfers between devices: 47.8 us -> 0 us
  starting transfers between devices: 45.3 us -> 0 us
  Pallas kernels: 0 us -> 36.5 us
  local copies, waits for them, and re-layouts: 19.8 us -> 1.69 us
  between operations: 14.3 us -> 0.65 us
  other arithmetic: 7.29 us -> 1.19 us
  matrix products: 5.41 us -> 0 us
    pallas_call x0 -> x1, Pallas kernels: none -> 36.5 us  [on_device(): pl.pallas_call(functools.partial(kernel, n, cap, float(limit)), out_shape...]
    ppermute x6 -> x0, starting transfers between devices: 23.9 us -> none  [shifted(): return lax.ppermute(array, axis, pairs)]
    all_to_all x2 -> x0, starting transfers between devices: 21.4 us -> none  [the longest x1 14 us: sorted_density(): lax.all_to_all(returned, 'blk', split_axis=0, concat_axis=0, tiled=True)]
    all_to_all x2 -> x0, waiting for transfers between devices: 21.2 us -> none  [the longest x1 21.2 us: sorted_density(): lax.all_to_all(packed, 'blk', split_axis=0, concat_axis=0, tiled=True)]
    psum x1 -> x0, waiting for transfers between devices: 19.2 us -> none  [on_device(): centroid = lax.psum(partial_sum, 'blk')]
    gather x4 -> x0, local copies, waits for them, and re-layouts: 8.25 us -> none  [the longest x2 4.29 us: sorted_density(): unit[sender]]
    scatter x3 -> x0, local copies, waits for them, and re-layouts: 7.81 us -> none  [the longest x1 2.92 us: sorted_density(): jnp.zeros((devices * capacity,), jnp.float32)]
    ppermute x6 -> x0, waiting for transfers between devices: 7.4 us -> none  [shifted(): return lax.ppermute(array, axis, pairs)]
  transfers between devices with their start and end apart: 9 -> 0, of which waited for: 5 -> 0; matrix products, arithmetic and copies ran while one was open for 9% -> 0% of each run, Pallas kernels for 0% -> 0%
where the time goes in v1:
time: 40.4 us; the launch traced here: 40 us
  Pallas kernels  36.5 us (90%)
  local copies, waits for them, and re-layouts  1.69 us (4%)
  other arithmetic  1.19 us (3%)
  between operations  0.65 us (2%)
    pallas_call x1, Pallas kernels, on_device(): pl.pallas_call(functools.partial(kernel, n, cap, float(limit)), out_shape...  36.5 us
    pallas_call x2, other arithmetic, on_device(): pl.pallas_call(functools.partial(kernel, n, cap, float(limit)), out_shape...  1.19 us
    unnamed x4, local copies, waits for them, and re-layouts  1 us

profile of v1, /device:TPU:0, one launch (start us, length us, event | category | flops | bytes accessed | tf_op | source)
XLA Modules:
  0.0 40.0 jit_solution(859836483305927535)
XLA Ops:
  0.6 0.0 copy-start.1
  0.6 0.7 %broadcast_in_dim.6.ids_ref = s32[1,384]{1,0:T(1,128)S(1)} reshape(s32[384]{0:T(512)} %param.4) | data formatting | bytes 3072 | tf_op jit(solution)/shard_map/broadcast_in_dim | solution.py:227
  1.3 0.0 copy-done.1
  1.3 0.0 copy-start
  1.3 1.0 %copy-done = bf16[384,512]{1,0:T(8,128)(2,1)S(1)} copy-done((bf16[384,512]{1,0:T(8,128)(2,1)S(1)}, bf16[384,512]{1,0:T(8,128)(2,1)}, u32[]{:S(2)}) %copy-start) | copy-done | bytes 393240
  2.3 36.5 %shard_map.50 = (f32[1,384]{1,0:T(1,128)S(1)}, f32[1,384]{1,0:T(1,128)S(1)}) custom-call(bf16[384,512]{1,0:T(8,128)(2,1)S(1)} %copy-done, s32[1,384]{1,0:T(1,128)S(1)} %broadcast_in_dim.6.ids_ref, s32[1,64]{1,0:T(1,128)S(1)} %bitcast.1), custom_call_target="tpu_custom_call" | custom-call | flops 4000000000 | bytes 1000000 | tf_op jit(solution)/shard_map/pallas_call | solution.py:208
  38.8 0.6 %reduce = f32[384]{0:T(512)} reduce(f32[1,384]{1,0:T(1,128)S(1)} %get-tuple-element.4, f32[]{:T(128)} %constant), dimensions={0}, to_apply=%get-tuple-element.4.reduce_sub_computation | reduce | bytes 3076 | tf_op jit(solution)/shard_map/pallas_call | solution.py:208
  39.4 0.6 %reduce.1 = f32[384]{0:T(512)} reduce(f32[1,384]{1,0:T(1,128)S(1)} %get-tuple-element.5, f32[]{:T(128)} %constant), dimensions={0}, to_apply=%get-tuple-element.5.reduce_sub_computation | reduce | bytes 3076 | tf_op jit(solution)/shard_map/pallas_call | solution.py:208
Async XLA Ops:
  0.6 0.7 %copy-start.1 = (s32[64]{0:T(128)S(1)}, s32[64]{0:T(128)}, u32[]{:S(2)}) copy-start(s32[64]{0:T(128)} %param.5) | copy-start | bytes 772
  1.3 1.0 %copy-start = (bf16[384,512]{1,0:T(8,128)(2,1)S(1)}, bf16[384,512]{1,0:T(8,128)(2,1)}, u32[]{:S(2)}) copy-start(bf16[384,512]{1,0:T(8,128)(2,1)} %emb_ref.1) | copy-start | bytes 1179652

commit v2 on v1

v2 whole, which is shorter than its diff:
```python
import functools

import jax
import jax.numpy as jnp
from jax import lax
from jax.experimental import pallas as pl
from jax.experimental.pallas import tpu as pltpu
from jax.sharding import PartitionSpec as P

SOFTMAX_TEMP = 0.1
EPSILON = 1e-06
LANES = 128
MESH = pl.DeviceIdType.MESH
F32 = jnp.float32
BF16 = jnp.bfloat16
NT = (((1,), (1,)), ((), ()))


def iota(shape, dim):
    return lax.broadcasted_iota(jnp.int32, shape, dim)


def loop(count, body):
    if count <= 8:
        for step in range(count):
            body(step)
    else:
        lax.fori_loop(0, count, lambda step, carry: (body(step), carry)[1], 0)


def kernel(n, cap, limit, emb_hbm, ids_hbm, sizes_hbm, out_ref,
           emb, ids_ref, sizes_ref, packed, packed_lab, own, other, own_lab, other_lab, ret, ret_in, addr_ref,
           acc_dens, acc_cent, emb_sem, ids_sem, sizes_sem,
           send, recv, send_lab, recv_lab, fsend, frecv, fsend_lab, frecv_lab, rsend, rrecv):
    bins = n // 2
    rows, width = emb.shape
    clusters = sizes_ref.shape[0]
    me = lax.axis_index("blk")
    chip = lax.div(me, 2)
    core = lax.rem(me, 2)
    partner = 2 * chip + 1 - core

    def distance(place):
        if isinstance(place, int) and place == 0:
            return 0
        return bins // 2 + (2 * lax.rem(place, 2) - 1) * lax.div(place, 2)

    def peer(place):
        return 2 * lax.rem(chip + distance(place), bins) + core

    def back(place):
        return 2 * lax.rem(chip + bins - distance(place), bins) + core

    fetch = pltpu.make_async_copy(emb_hbm, emb, emb_sem)
    fetch_ids = pltpu.make_async_copy(ids_hbm, ids_ref, ids_sem)
    fetch_sizes = pltpu.make_async_copy(sizes_hbm, sizes_ref, sizes_sem)
    fetch_sizes.start()
    fetch_ids.start()
    fetch.start()
    barrier = pltpu.get_barrier_semaphore()
    pl.semaphore_signal(barrier, inc=1, device_id={"blk": partner}, device_id_type=MESH)
    loop(bins - 1, lambda s: pl.semaphore_signal(
        barrier, inc=1, device_id={"blk": peer(s + 1)}, device_id_type=MESH))

    fetch_sizes.wait()
    sizes_row = sizes_ref[...].reshape(1, clusters).astype(F32)
    above = iota((clusters, clusters), 0)
    along = iota((clusters, clusters), 1)
    ends = jnp.sum(jnp.where(along <= above, sizes_row, 0.0), axis=1, keepdims=True)
    sizes = jnp.sum(jnp.where(along == above, sizes_row, 0.0), axis=1, keepdims=True)
    starts = ends - sizes
    edge = jnp.zeros((1, 1), F32)
    bin_of = jnp.zeros((clusters, 1), F32)
    for _ in range(bins - 1):
        edge = jnp.max(jnp.where(ends <= edge + limit, ends, 0.0), axis=0, keepdims=True)
        bin_of += jnp.where(starts >= edge, 1.0, 0.0)

    fetch_ids.wait()
    ids = ids_ref[...].reshape(1, rows)
    member = iota((clusters, rows), 0) == ids
    bin_row = jnp.sum(jnp.where(member, bin_of, 0.0), axis=0, keepdims=True)
    size_row = jnp.sum(jnp.where(member, sizes, 0.0), axis=0, keepdims=True)
    shown = max(bins, 8)
    in_bin = iota((shown, rows), 0).astype(F32) == bin_row
    before = jnp.where(iota((rows, rows), 0) < iota((rows, rows), 1), 1.0, 0.0).astype(BF16)
    rank = jnp.dot(jnp.where(in_bin, 1.0, 0.0).astype(BF16), before, preferred_element_type=F32)
    slot = jnp.sum(jnp.where(in_bin, rank, 0.0), axis=0, keepdims=True)
    address = (bin_row * LANES + slot).astype(jnp.int32)
    addr_ref[...] = jnp.broadcast_to(address, addr_ref.shape)
    label_rows = jnp.broadcast_to((ids + 1).astype(F32), (8, rows)).astype(BF16)

    fetch.wait()
    values = emb[...].astype(F32)
    scale = lax.rsqrt(jnp.mean(values * values, axis=1, keepdims=True) + EPSILON)
    unit = (values * (scale * width ** (-0.5))).astype(BF16)

    def hot(place):
        first = lax.rem(chip + distance(place), bins) * LANES
        return iota((LANES, rows), 0) + first == addr_ref[0:1, :]

    def data_copy(place):
        return pltpu.make_async_remote_copy(
            packed.at[place, pl.ds(0, cap)], own.at[place, pl.ds(0, cap)],
            send.at[place], recv.at[place], device_id={"blk": peer(place)}, device_id_type=MESH)

    def label_copy(place):
        return pltpu.make_async_remote_copy(
            packed_lab.at[place], own_lab.at[place], send_lab.at[place], recv_lab.at[place],
            device_id={"blk": peer(place)}, device_id_type=MESH)

    def forward_copy(place):
        return pltpu.make_async_remote_copy(
            own.at[place, pl.ds(0, cap)], other.at[place, pl.ds(0, cap)],
            fsend.at[place], frecv.at[place], device_id={"blk": partner}, device_id_type=MESH)

    def forward_label_copy(place):
        return pltpu.make_async_remote_copy(
            own_lab.at[place], other_lab.at[place], fsend_lab.at[place], frecv_lab.at[place],
            device_id={"blk": partner}, device_id_type=MESH)

    def return_copy(place):
        return pltpu.make_async_remote_copy(
            ret.at[place], ret_in.at[place], rsend.at[place], rrecv.at[place],
            device_id={"blk": back(place)}, device_id_type=MESH)

    def pack(place, rows_ref, lab_ref):
        one_hot = jnp.where(hot(place), 1.0, 0.0).astype(BF16)
        rows_ref[place] = jnp.dot(one_hot, unit, preferred_element_type=F32).astype(BF16)
        lab_ref[place] = lax.dot_general(label_rows, one_hot, NT, preferred_element_type=F32)

    pl.semaphore_wait(barrier, bins)

    def send_step(s):
        pack(s + 1, packed, packed_lab)
        label_copy(s + 1).start()
        data_copy(s + 1).start()

    loop(bins - 1, send_step)
    pack(0, own, own_lab)
    forward_label_copy(0).start()
    forward_copy(0).start()
    if cap < LANES:
        def clear(s):
            own[s + 1, cap:, :] = jnp.zeros((LANES - cap, width), BF16)
        loop(bins - 1, clear)

    def clear_sums(pair):
        acc_dens[pair] = jnp.zeros((8, 2 * LANES), F32)
        acc_cent[pair] = jnp.zeros((8, 2 * LANES), F32)

    loop(bins // 2, clear_sums)

    def take(place):
        label_copy(place).wait_recv()
        forward_label_copy(place).start()
        data_copy(place).wait_recv()
        forward_copy(place).start()

    def arrived(place):
        forward_label_copy(place).wait_recv()
        forward_copy(place).wait_recv()

    def tile(side, lab, left, right):
        left_rows = side[pl.ds(2 * left, 2), :cap, :].reshape(2 * cap, width)
        left_lab = jnp.concatenate(
            [lab[2 * left + half].T[:cap, 0:1] for half in range(2)], axis=0)
        right_rows = own[pl.ds(2 * right, 2)].reshape(2 * LANES, width)
        right_lab = jnp.concatenate(
            [own_lab[2 * right + half, 0:1, :] for half in range(2)], axis=1)
        cosine = lax.dot_general(left_rows, right_rows, NT, preferred_element_type=F32)
        same = left_lab == right_lab
        dens = jnp.where(same, jnp.exp(cosine * (1.0 / SOFTMAX_TEMP)), 0.0)
        cent = jnp.where(same, cosine, 0.0)
        acc_dens[right] += jnp.sum(dens.reshape(2 * cap // 8, 8, 2 * LANES), axis=0)
        acc_cent[right] += jnp.sum(cent.reshape(2 * cap // 8, 8, 2 * LANES), axis=0)

    def close(pair):
        dens = jnp.sum(acc_dens[pair], axis=0, keepdims=True)
        cent = jnp.sum(acc_cent[pair], axis=0, keepdims=True)
        for half in range(2):
            part = slice(half * LANES, (half + 1) * LANES)
            ret[2 * pair + half] = jnp.concatenate(
                [dens[:, part], cent[:, part], jnp.zeros((6, LANES), F32)], axis=0)

    def span(count, body):
        if isinstance(count, int):
            loop(count, body)
        else:
            lax.fori_loop(0, count, lambda step, carry: (body(step), carry)[1], 0)

    def group(pair):
        span(pair, lambda q: tile(own, own_lab, pair, q))
        span(pair, lambda q: tile(own, own_lab, q, pair))
        tile(own, own_lab, pair, pair)
        span(pair, lambda q: tile(other, other_lab, q, pair))
        arrived(2 * pair)
        arrived(2 * pair + 1)

    def finish_group(pair):
        span(pair, lambda q: tile(other, other_lab, pair, q))
        tile(other, other_lab, pair, pair)

    pairs = bins // 2
    take(1)
    group(0)
    finish_group(0)

    def middle(s):
        take(2 * s + 2)
        take(2 * s + 3)
        group(s + 1)
        finish_group(s + 1)

    loop(pairs - 2, middle)
    last = pairs - 1
    take(2 * last)
    take(2 * last + 1)
    group(last)
    tile(other, other_lab, last, 0)
    close(0)
    ret_in[0] = ret[0]
    return_copy(1).start()

    def answer(s):
        tile(other, other_lab, last, s + 1)
        close(s + 1)
        return_copy(2 * s + 2).start()
        return_copy(2 * s + 3).start()

    loop(pairs - 1, answer)

    def gathered(place, total):
        values = ret_in[place].T
        mine = hot(place)
        return (total[0] + jnp.where(mine, values[:, 0:1], 0.0),
                total[1] + jnp.where(mine, values[:, 1:2], 0.0))

    none = jnp.zeros((LANES, rows), F32)
    total = gathered(0, (none, none))

    def collect(place, total):
        return_copy(place).wait_recv()
        return gathered(place, total)

    if bins <= 8:
        for place in range(1, bins):
            total = collect(place, total)
    else:
        total = lax.fori_loop(1, bins, collect, total)
    dens = jnp.sum(total[0], axis=0, keepdims=True) / size_row
    cent = jnp.sum(total[1], axis=0, keepdims=True) / size_row
    out_ref[...] = jnp.concatenate([jnp.log(dens), cent, jnp.zeros((6, rows), F32)], axis=0)

    def finish(s):
        data_copy(s + 1).wait_send()
        label_copy(s + 1).wait_send()
        return_copy(s + 1).wait_send()

    loop(bins - 1, finish)

    def finish_forward(s):
        forward_copy(s).wait_send()
        forward_label_copy(s).wait_send()

    loop(bins, finish_forward)


def on_device(embeddings, cluster_ids, cluster_sizes):
    n = lax.axis_size("blk")
    rows, width = embeddings.shape
    bins = n // 2
    total = rows * n
    limit = max(2 * total // bins, total * 5 // 32)
    cap = -(-(-(-limit // n)) // 16) * 16
    vmem = pl.BlockSpec(memory_space=pltpu.VMEM)
    hbm = pl.BlockSpec(memory_space=pltpu.HBM)
    dma = pltpu.SemaphoreType.DMA((bins,))
    out = pl.pallas_call(
        functools.partial(kernel, n, cap, float(limit)),
        out_shape=jax.ShapeDtypeStruct((8, rows), F32),
        in_specs=[hbm] * 3,
        out_specs=vmem,
        scratch_shapes=[
            pltpu.VMEM((rows, width), BF16),
            pltpu.VMEM(cluster_ids.shape, jnp.int32),
            pltpu.VMEM(cluster_sizes.shape, jnp.int32),
            pltpu.VMEM((bins, LANES, width), BF16),
            pltpu.VMEM((bins, 8, LANES), F32),
            pltpu.VMEM((bins, LANES, width), BF16),
            pltpu.VMEM((bins, LANES, width), BF16),
            pltpu.VMEM((bins, 8, LANES), F32),
            pltpu.VMEM((bins, 8, LANES), F32),
            pltpu.VMEM((bins, 8, LANES), F32),
            pltpu.VMEM((bins, 8, LANES), F32),
            pltpu.VMEM((8, rows), jnp.int32),
            pltpu.VMEM((bins // 2, 8, 2 * LANES), F32),
            pltpu.VMEM((bins // 2, 8, 2 * LANES), F32),
            pltpu.SemaphoreType.DMA,
            pltpu.SemaphoreType.DMA,
            pltpu.SemaphoreType.DMA,
        ] + [dma] * 10,
        compiler_params=pltpu.CompilerParams(
            collective_id=0, has_side_effects=True, vmem_limit_bytes=48 * 1024 * 1024),
        cost_estimate=pl.CostEstimate(flops=4 * 10 ** 9, bytes_accessed=10 ** 6, transcendentals=0),
    )(embeddings, cluster_ids, cluster_sizes)
    return out[0], out[1]


def solution(mesh):
    in_specs = (P(("groups", "blk"), None), P(("groups", "blk")), P("groups"))
    out_specs = (P(("groups", "blk")), P(("groups", "blk")))
    return jax.shard_map(
        on_device, mesh=mesh, in_specs=in_specs, out_specs=out_specs, check_vma=False
    )
```

time: 40.4 us -> 39.2 us (0.970)
  local copies, waits for them, and re-layouts: 1.69 us -> 2.93 us
  other arithmetic: 1.19 us -> 0 us
  Pallas kernels: 36.5 us -> 35.4 us
    unnamed x4 -> x6, local copies, waits for them, and re-layouts: 1 us -> 2.32 us
    pallas_call x2 -> x0, other arithmetic: 1.19 us -> none  [on_device(): pl.pallas_call(functools.partial(kernel, n, cap, float(limit)), out_shape...]
    pallas_call x1, Pallas kernels: 36.5 us -> 35.4 us  [on_device(): pl.pallas_call(functools.partial(kernel, n, cap, float(limit)), out_shape...]
    broadcast_in_dim x1 -> x0, local copies, waits for them, and re-layouts: 0.69 us -> none  [on_device(): cluster_ids[None, :]]
    slice x0 -> x1, local copies, waits for them, and re-layouts: none -> 0.6 us  [on_device(): return (out[0], out[1])]
where the time goes in v2:
time: 39.2 us; the launch traced here: 39 us
  Pallas kernels  35.4 us (90%)
  local copies, waits for them, and re-layouts  2.93 us (7%)
  between operations  0.65 us (2%)
    pallas_call x1, Pallas kernels, on_device(): pl.pallas_call(functools.partial(kernel, n, cap, float(limit)), out_shape...  35.4 us
    unnamed x6, local copies, waits for them, and re-layouts  2.32 us

profile of v2, /device:TPU:0, one launch (start us, length us, event | category | flops | bytes accessed | tf_op | source)
XLA Modules:
  0.0 39.0 jit_solution(12750370155956774510)
XLA Ops:
  0.6 0.0 copy-start
  0.6 1.0 %copy-done = bf16[384,512]{1,0:T(8,128)(2,1)S(1)} copy-done((bf16[384,512]{1,0:T(8,128)(2,1)S(1)}, bf16[384,512]{1,0:T(8,128)(2,1)}, u32[]{:S(2)}) %copy-start) | copy-done | bytes 393240
  1.6 0.0 copy-start.1
  1.6 0.7 %copy-done.1 = s32[384]{0:T(512)S(1)} copy-done((s32[384]{0:T(512)S(1)}, s32[384]{0:T(512)}, u32[]{:S(2)}) %copy-start.1) | copy-done | bytes 1560
  2.3 0.0 copy-start.2
  2.3 0.7 %copy-done.2 = s32[64]{0:T(128)S(1)} copy-done((s32[64]{0:T(128)S(1)}, s32[64]{0:T(128)}, u32[]{:S(2)}) %copy-start.2) | copy-done | bytes 280
  3.0 35.4 %shard_map.50 = f32[8,384]{1,0:T(8,128)S(1)} custom-call(bf16[384,512]{1,0:T(8,128)(2,1)S(1)} %copy-done, s32[384]{0:T(512)S(1)} %copy-done.1, s32[64]{0:T(128)S(1)} %copy-done.2), custom_call_target="tpu_custom_call" | custom-call | flops 4000000000 | bytes 1000000 | tf_op jit(solution)/shard_map/pallas_call | solution.py:278
  38.4 0.6 %slice_reduce_fusion = (f32[384]{0:T(512)}, f32[384]{0:T(512)}) fusion(f32[8,384]{1,0:T(8,128)S(1)} %shard_map.50), kind=kLoop, calls=%fused_computation | loop fusion | bytes 6144 | tf_op jit(solution)/shard_map/slice | solution.py:306
Async XLA Ops:
  0.6 1.0 %copy-start = (bf16[384,512]{1,0:T(8,128)(2,1)S(1)}, bf16[384,512]{1,0:T(8,128)(2,1)}, u32[]{:S(2)}) copy-start(bf16[384,512]{1,0:T(8,128)(2,1)} %emb_hbm.1) | copy-start | bytes 1179652
  1.6 0.7 %copy-start.1 = (s32[384]{0:T(512)S(1)}, s32[384]{0:T(512)}, u32[]{:S(2)}) copy-start(s32[384]{0:T(512)} %ids_hbm.1) | copy-start | bytes 4612
  2.3 0.7 %copy-start.2 = (s32[64]{0:T(128)S(1)}, s32[64]{0:T(128)}, u32[]{:S(2)}) copy-start(s32[64]{0:T(128)} %sizes_hbm.1) | copy-start | bytes 772

commit v3 on v2

--- a/solution.py
+++ b/solution.py
@@ -28,7 +28,7 @@
         lax.fori_loop(0, count, lambda step, carry: (body(step), carry)[1], 0)
 
 
-def kernel(n, cap, limit, emb_hbm, ids_hbm, sizes_hbm, out_ref,
+def kernel(n, cap, caps, chips, limit, emb_hbm, ids_hbm, sizes_hbm, out_ref,
            emb, ids_ref, sizes_ref, packed, packed_lab, own, other, own_lab, other_lab, ret, ret_in, addr_ref,
            acc_dens, acc_cent, emb_sem, ids_sem, sizes_sem,
            send, recv, send_lab, recv_lab, fsend, frecv, fsend_lab, frecv_lab, rsend, rrecv):
@@ -69,23 +69,36 @@
     ends = jnp.sum(jnp.where(along <= above, sizes_row, 0.0), axis=1, keepdims=True)
     sizes = jnp.sum(jnp.where(along == above, sizes_row, 0.0), axis=1, keepdims=True)
     starts = ends - sizes
+    shown = max(bins, 8)
     edge = jnp.zeros((1, 1), F32)
     bin_of = jnp.zeros((clusters, 1), F32)
-    for _ in range(bins - 1):
+    load = jnp.zeros((shown, 1), F32)
+    load_row = jnp.zeros((1, LANES), F32)
+    for index in range(bins):
+        filled = edge
         edge = jnp.max(jnp.where(ends <= edge + limit, ends, 0.0), axis=0, keepdims=True)
         bin_of += jnp.where(starts >= edge, 1.0, 0.0)
+        load = jnp.where(iota((shown, 1), 0) == index, edge - filled, load)
+        load_row = jnp.where(iota((1, LANES), 1) == index, edge - filled, load_row)
+    earlier = iota((shown, LANES), 1) < iota((shown, LANES), 0)
+    ahead = (load_row > load) | ((load_row == load) & earlier)
+    ahead = ahead & (iota((shown, LANES), 1) < bins)
+    order = jnp.sum(jnp.where(ahead, 1.0, 0.0), axis=1, keepdims=True)
+    home = jnp.zeros((shown, 1), F32)
+    for place in range(bins):
+        home = jnp.where(order == place, float(chips[place]), home)
 
     fetch_ids.wait()
     ids = ids_ref[...].reshape(1, rows)
     member = iota((clusters, rows), 0) == ids
     bin_row = jnp.sum(jnp.where(member, bin_of, 0.0), axis=0, keepdims=True)
     size_row = jnp.sum(jnp.where(member, sizes, 0.0), axis=0, keepdims=True)
-    shown = max(bins, 8)
     in_bin = iota((shown, rows), 0).astype(F32) == bin_row
     before = jnp.where(iota((rows, rows), 0) < iota((rows, rows), 1), 1.0, 0.0).astype(BF16)
     rank = jnp.dot(jnp.where(in_bin, 1.0, 0.0).astype(BF16), before, preferred_element_type=F32)
     slot = jnp.sum(jnp.where(in_bin, rank, 0.0), axis=0, keepdims=True)
-    address = (bin_row * LANES + slot).astype(jnp.int32)
+    home_row = jnp.sum(jnp.where(in_bin, home, 0.0), axis=0, keepdims=True)
+    address = (home_row * LANES + slot).astype(jnp.int32)
     addr_ref[...] = jnp.broadcast_to(address, addr_ref.shape)
     label_rows = jnp.broadcast_to((ids + 1).astype(F32), (8, rows)).astype(BF16)
 
@@ -98,9 +111,15 @@
         first = lax.rem(chip + distance(place), bins) * LANES
         return iota((LANES, rows), 0) + first == addr_ref[0:1, :]
 
-    def data_copy(place):
-        return pltpu.make_async_remote_copy(
-            packed.at[place, pl.ds(0, cap)], own.at[place, pl.ds(0, cap)],
+    def sized(where, act):
+        for size in sorted(set(caps)):
+            match = functools.reduce(
+                jnp.logical_or, [where == chips[r] for r in range(bins) if caps[r] == size])
+            pl.when(match)(functools.partial(act, size))
+
+    def data_copy(place, size):
+        return pltpu.make_async_remote_copy(
+            packed.at[place, pl.ds(0, size)], own.at[place, pl.ds(0, size)],
             send.at[place], recv.at[place], device_id={"blk": peer(place)}, device_id_type=MESH)
 
     def label_copy(place):
@@ -108,9 +127,9 @@
             packed_lab.at[place], own_lab.at[place], send_lab.at[place], recv_lab.at[place],
             device_id={"blk": peer(place)}, device_id_type=MESH)
 
-    def forward_copy(place):
-        return pltpu.make_async_remote_copy(
-            own.at[place, pl.ds(0, cap)], other.at[place, pl.ds(0, cap)],
+    def forward_copy(place, size):
+        return pltpu.make_async_remote_copy(
+            own.at[place, pl.ds(0, size)], other.at[place, pl.ds(0, size)],
             fsend.at[place], frecv.at[place], device_id={"blk": partner}, device_id_type=MESH)
 
     def forward_label_copy(place):
@@ -133,16 +152,24 @@
     def send_step(s):
         pack(s + 1, packed, packed_lab)
         label_copy(s + 1).start()
-        data_copy(s + 1).start()
+        sized(lax.div(peer(s + 1), 2), lambda size: data_copy(s + 1, size).start())
 
     loop(bins - 1, send_step)
     pack(0, own, own_lab)
     forward_label_copy(0).start()
-    forward_copy(0).start()
-    if cap < LANES:
-        def clear(s):
-            own[s + 1, cap:, :] = jnp.zeros((LANES - cap, width), BF16)
-        loop(bins - 1, clear)
+    sized(chip, lambda size: forward_copy(0, size).start())
+
+    def clear(size):
+        def step(s):
+            if size < LANES:
+                own[s + 1, size:, :] = jnp.zeros((LANES - size, width), BF16)
+            if size < cap:
+                other[s, size:cap, :] = jnp.zeros((cap - size, width), BF16)
+        loop(bins - 1, step)
+        if size < cap:
+            other[bins - 1, size:cap, :] = jnp.zeros((cap - size, width), BF16)
+
+    sized(chip, clear)
 
     def clear_sums(pair):
         acc_dens[pair] = jnp.zeros((8, 2 * LANES), F32)
@@ -153,12 +180,16 @@
     def take(place):
         label_copy(place).wait_recv()
         forward_label_copy(place).start()
-        data_copy(place).wait_recv()
-        forward_copy(place).start()
+
+        def go(size):
+            data_copy(place, size).wait_recv()
+            forward_copy(place, size).start()
+
+        sized(chip, go)
 
     def arrived(place):
         forward_label_copy(place).wait_recv()
-        forward_copy(place).wait_recv()
+        sized(chip, lambda size: forward_copy(place, size).wait_recv())
 
     def tile(side, lab, left, right):
         left_rows = side[pl.ds(2 * left, 2), :cap, :].reshape(2 * cap, width)
@@ -252,14 +283,14 @@
     out_ref[...] = jnp.concatenate([jnp.log(dens), cent, jnp.zeros((6, rows), F32)], axis=0)
 
     def finish(s):
-        data_copy(s + 1).wait_send()
+        sized(lax.div(peer(s + 1), 2), lambda size: data_copy(s + 1, size).wait_send())
         label_copy(s + 1).wait_send()
         return_copy(s + 1).wait_send()
 
     loop(bins - 1, finish)
 
     def finish_forward(s):
-        forward_copy(s).wait_send()
+        sized(chip, lambda size: forward_copy(s, size).wait_send())
         forward_label_copy(s).wait_send()
 
     loop(bins, finish_forward)
@@ -271,12 +302,17 @@
     bins = n // 2
     total = rows * n
     limit = max(2 * total // bins, total * 5 // 32)
-    cap = -(-(-(-limit // n)) // 16) * 16
+    caps = [-(-min(-(-limit // n), -(-rows // (r + 1))) // 16) * 16 for r in range(bins)]
+    cap = caps[0]
+    chips = []
+    for r in range(bins // 2):
+        low, high = bins // 2 - 1 - r, bins // 2 + r
+        chips += [low, high] if r % 2 == 0 else [high, low]
     vmem = pl.BlockSpec(memory_space=pltpu.VMEM)
     hbm = pl.BlockSpec(memory_space=pltpu.HBM)
     dma = pltpu.SemaphoreType.DMA((bins,))
     out = pl.pallas_call(
-        functools.partial(kernel, n, cap, float(limit)),
+        functools.partial(kernel, n, cap, tuple(caps), tuple(chips), float(limit)),
         out_shape=jax.ShapeDtypeStruct((8, rows), F32),
         in_specs=[hbm] * 3,
         out_specs=vmem,
@@ -300,7 +336,7 @@
             pltpu.SemaphoreType.DMA,
         ] + [dma] * 10,
         compiler_params=pltpu.CompilerParams(
-            collective_id=0, has_side_effects=True, vmem_limit_bytes=48 * 1024 * 1024),
+            collective_id=0, has_side_effects=True, vmem_limit_bytes=64 * 1024 * 1024 - 128 * 1024),
         cost_estimate=pl.CostEstimate(flops=4 * 10 ** 9, bytes_accessed=10 ** 6, transcendentals=0),
     )(embeddings, cluster_ids, cluster_sizes)
     return out[0], out[1]

time: 39.2 us -> 35.3 us (0.901)
  Pallas kernels: 35.4 us -> 33 us
  local copies, waits for them, and re-layouts: 2.93 us -> 1.38 us
    pallas_call x1, Pallas kernels: 35.4 us -> 33 us  [on_device(): pl.pallas_call(functools.partial(kernel, n, cap, tuple(caps), tuple(chips...]
    unnamed x6 -> x0, local copies, waits for them, and re-layouts: 2.32 us -> none
    slice x1, local copies, waits for them, and re-layouts: 0.6 us -> 1.38 us  [on_device(): return (out[0], out[1])]
where the time goes in v3:
time: 35.3 us; the launch traced here: 35 us
  Pallas kernels  33 us (93%)
  local copies, waits for them, and re-layouts  1.38 us (4%)
  between operations  0.64 us (2%)
    pallas_call x1, Pallas kernels, on_device(): pl.pallas_call(functools.partial(kernel, n, cap, tuple(caps), tuple(chips...  33 us
    slice x1, local copies, waits for them, and re-layouts, on_device(): return (out[0], out[1])  1.38 us

profile of v3, /device:TPU:0, one launch (start us, length us, event | category | flops | bytes accessed | tf_op | source)
XLA Modules:
  0.0 35.0 jit_solution(2804684101117027473)
XLA Ops:
  0.6 33.0 %shard_map.50 = f32[8,384]{1,0:T(8,128)} custom-call(bf16[384,512]{1,0:T(8,128)(2,1)} %emb_hbm.1, s32[384]{0:T(512)} %ids_hbm.1, s32[64]{0:T(128)} %sizes_hbm.1), custom_call_target="tpu_custom_call" | custom-call | flops 4000000000 | bytes 1000000 | tf_op jit(solution)/shard_map/pallas_call | solution.py:314
  33.7 1.4 %slice_reduce_fusion = (f32[384]{0:T(512)}, f32[384]{0:T(512)}) fusion(f32[8,384]{1,0:T(8,128)} %shard_map.50), kind=kLoop, calls=%fused_computation | loop fusion | bytes 6144 | tf_op jit(solution)/shard_map/slice | solution.py:342

commit v4 on v3

--- a/solution.py
+++ b/solution.py
@@ -43,7 +43,8 @@
     def distance(place):
         if isinstance(place, int) and place == 0:
             return 0
-        return bins // 2 + (2 * lax.rem(place, 2) - 1) * lax.div(place, 2)
+        turn = bins - place
+        return bins // 2 + (2 * lax.rem(turn, 2) - 1) * lax.div(turn, 2)
 
     def peer(place):
         return 2 * lax.rem(chip + distance(place), bins) + core
@@ -150,9 +151,10 @@
     pl.semaphore_wait(barrier, bins)
 
     def send_step(s):
-        pack(s + 1, packed, packed_lab)
-        label_copy(s + 1).start()
-        sized(lax.div(peer(s + 1), 2), lambda size: data_copy(s + 1, size).start())
+        place = bins - 1 - s
+        pack(place, packed, packed_lab)
+        label_copy(place).start()
+        sized(lax.div(peer(place), 2), lambda size: data_copy(place, size).start())
 
     loop(bins - 1, send_step)
     pack(0, own, own_lab)

time: 35.3 us -> 36.5 us (1.034)
  Pallas kernels: 33 us -> 34.3 us
    pallas_call x1, Pallas kernels: 33 us -> 34.3 us  [on_device(): pl.pallas_call(functools.partial(kernel, n, cap, tuple(caps), tuple(chips...]
where the time goes in v4:
time: 36.5 us; the launch traced here: 36.3 us
  Pallas kernels  34.3 us (94%)
  local copies, waits for them, and re-layouts  1.38 us (4%)
  between operations  0.64 us (2%)
    pallas_call x1, Pallas kernels, on_device(): pl.pallas_call(functools.partial(kernel, n, cap, tuple(caps), tuple(chips...  34.3 us
    slice x1, local copies, waits for them, and re-layouts, on_device(): return (out[0], out[1])  1.38 us

profile of v4, /device:TPU:0, one launch (start us, length us, event | category | flops | bytes accessed | tf_op | source)
XLA Modules:
  0.0 36.3 jit_solution(4694822409670911751)
XLA Ops:
  0.6 34.3 %shard_map.50 = f32[8,384]{1,0:T(8,128)} custom-call(bf16[384,512]{1,0:T(8,128)(2,1)} %emb_hbm.1, s32[384]{0:T(512)} %ids_hbm.1, s32[64]{0:T(128)} %sizes_hbm.1), custom_call_target="tpu_custom_call" | custom-call | flops 4000000000 | bytes 1000000 | tf_op jit(solution)/shard_map/pallas_call | solution.py:316
  34.9 1.4 %slice_reduce_fusion = (f32[384]{0:T(512)}, f32[384]{0:T(512)}) fusion(f32[8,384]{1,0:T(8,128)} %shard_map.50), kind=kLoop, calls=%fused_computation | loop fusion | bytes 6144 | tf_op jit(solution)/shard_map/slice | solution.py:344

commit v5 on v3

--- a/solution.py
+++ b/solution.py
@@ -40,16 +40,28 @@
     core = lax.rem(me, 2)
     partner = 2 * chip + 1 - core
 
-    def distance(place):
+    def turn(place):
         if isinstance(place, int) and place == 0:
-            return 0
-        return bins // 2 + (2 * lax.rem(place, 2) - 1) * lax.div(place, 2)
+            return jnp.int32(0)
+        place = jnp.int32(place)
+        half = lax.div(place, 2)
+        odd = lax.rem(place, 2)
+        first = odd * (bins // 2 + half) + (1 - odd) * half
+        second = odd * (half + 1) + (1 - odd) * (bins // 2 + half - 1)
+        at_end = lax.div(place, bins - 1)
+        second = at_end * (bins - 1) + (1 - at_end) * second
+        return first + core * (second - first)
+
+    def facing(place):
+        change, other_chip, bit = turn(place), chip, 1
+        while bit < bins:
+            flip = lax.rem(lax.div(change, bit), 2)
+            other_chip = other_chip + flip * bit * (1 - 2 * lax.rem(lax.div(chip, bit), 2))
+            bit *= 2
+        return other_chip
 
     def peer(place):
-        return 2 * lax.rem(chip + distance(place), bins) + core
-
-    def back(place):
-        return 2 * lax.rem(chip + bins - distance(place), bins) + core
+        return 2 * facing(place) + core
 
     fetch = pltpu.make_async_copy(emb_hbm, emb, emb_sem)
     fetch_ids = pltpu.make_async_copy(ids_hbm, ids_ref, ids_sem)
@@ -108,7 +120,7 @@
     unit = (values * (scale * width ** (-0.5))).astype(BF16)
 
     def hot(place):
-        first = lax.rem(chip + distance(place), bins) * LANES
+        first = facing(place) * LANES
         return iota((LANES, rows), 0) + first == addr_ref[0:1, :]
 
     def sized(where, act):
@@ -140,7 +152,7 @@
     def return_copy(place):
         return pltpu.make_async_remote_copy(
             ret.at[place], ret_in.at[place], rsend.at[place], rrecv.at[place],
-            device_id={"blk": back(place)}, device_id_type=MESH)
+            device_id={"blk": peer(place)}, device_id_type=MESH)
 
     def pack(place, rows_ref, lab_ref):
         one_hot = jnp.where(hot(place), 1.0, 0.0).astype(BF16)
@@ -152,7 +164,7 @@
     def send_step(s):
         pack(s + 1, packed, packed_lab)
         label_copy(s + 1).start()
-        sized(lax.div(peer(s + 1), 2), lambda size: data_copy(s + 1, size).start())
+        sized(facing(s + 1), lambda size: data_copy(s + 1, size).start())
 
     loop(bins - 1, send_step)
     pack(0, own, own_lab)
@@ -283,7 +295,7 @@
     out_ref[...] = jnp.concatenate([jnp.log(dens), cent, jnp.zeros((6, rows), F32)], axis=0)
 
     def finish(s):
-        sized(lax.div(peer(s + 1), 2), lambda size: data_copy(s + 1, size).wait_send())
+        sized(facing(s + 1), lambda size: data_copy(s + 1, size).wait_send())
         label_copy(s + 1).wait_send()
         return_copy(s + 1).wait_send()
 

time: 35.3 us -> 32.9 us (0.932)
  Pallas kernels: 33 us -> 30.6 us
    pallas_call x1, Pallas kernels: 33 us -> 30.6 us  [on_device(): pl.pallas_call(functools.partial(kernel, n, cap, tuple(caps), tuple(chips...]
where the time goes in v5:
time: 32.9 us; the launch traced here: 32.6 us
  Pallas kernels  30.6 us (93%)
  local copies, waits for them, and re-layouts  1.38 us (4%)
  between operations  0.64 us (2%)
    pallas_call x1, Pallas kernels, on_device(): pl.pallas_call(functools.partial(kernel, n, cap, tuple(caps), tuple(chips...  30.6 us
    slice x1, local copies, waits for them, and re-layouts, on_device(): return (out[0], out[1])  1.38 us

profile of v5, /device:TPU:0, one launch (start us, length us, event | category | flops | bytes accessed | tf_op | source)
XLA Modules:
  0.0 32.6 jit_solution(6849866612637525748)
XLA Ops:
  0.6 30.6 %shard_map.50 = f32[8,384]{1,0:T(8,128)} custom-call(bf16[384,512]{1,0:T(8,128)(2,1)} %emb_hbm.1, s32[384]{0:T(512)} %ids_hbm.1, s32[64]{0:T(128)} %sizes_hbm.1), custom_call_target="tpu_custom_call" | custom-call | flops 4000000000 | bytes 1000000 | tf_op jit(solution)/shard_map/pallas_call | solution.py:326
  31.3 1.4 %slice_reduce_fusion = (f32[384]{0:T(512)}, f32[384]{0:T(512)}) fusion(f32[8,384]{1,0:T(8,128)} %shard_map.50), kind=kLoop, calls=%fused_computation | loop fusion | bytes 6144 | tf_op jit(solution)/shard_map/slice | solution.py:354

commit v6 on v5

--- a/solution.py
+++ b/solution.py
@@ -30,7 +30,7 @@
 
 def kernel(n, cap, caps, chips, limit, emb_hbm, ids_hbm, sizes_hbm, out_ref,
            emb, ids_ref, sizes_ref, packed, packed_lab, own, other, own_lab, other_lab, ret, ret_in, addr_ref,
-           acc_dens, acc_cent, emb_sem, ids_sem, sizes_sem,
+           acc_dens, acc_cent, before_ref, emb_sem, ids_sem, sizes_sem,
            send, recv, send_lab, recv_lab, fsend, frecv, fsend_lab, frecv_lab, rsend, rrecv):
     bins = n // 2
     rows, width = emb.shape
@@ -73,6 +73,9 @@
     pl.semaphore_signal(barrier, inc=1, device_id={"blk": partner}, device_id_type=MESH)
     loop(bins - 1, lambda s: pl.semaphore_signal(
         barrier, inc=1, device_id={"blk": peer(s + 1)}, device_id_type=MESH))
+
+    before_ref[...] = jnp.where(
+        iota((rows, rows), 0) < iota((rows, rows), 1), 1.0, 0.0).astype(BF16)
 
     fetch_sizes.wait()
     sizes_row = sizes_ref[...].reshape(1, clusters).astype(F32)
@@ -106,8 +109,7 @@
     bin_row = jnp.sum(jnp.where(member, bin_of, 0.0), axis=0, keepdims=True)
     size_row = jnp.sum(jnp.where(member, sizes, 0.0), axis=0, keepdims=True)
     in_bin = iota((shown, rows), 0).astype(F32) == bin_row
-    before = jnp.where(iota((rows, rows), 0) < iota((rows, rows), 1), 1.0, 0.0).astype(BF16)
-    rank = jnp.dot(jnp.where(in_bin, 1.0, 0.0).astype(BF16), before, preferred_element_type=F32)
+    rank = jnp.dot(jnp.where(in_bin, 1.0, 0.0).astype(BF16), before_ref[...], preferred_element_type=F32)
     slot = jnp.sum(jnp.where(in_bin, rank, 0.0), axis=0, keepdims=True)
     home_row = jnp.sum(jnp.where(in_bin, home, 0.0), axis=0, keepdims=True)
     address = (home_row * LANES + slot).astype(jnp.int32)
@@ -159,10 +161,12 @@
         rows_ref[place] = jnp.dot(one_hot, unit, preferred_element_type=F32).astype(BF16)
         lab_ref[place] = lax.dot_general(label_rows, one_hot, NT, preferred_element_type=F32)
 
+    pack(1, packed, packed_lab)
     pl.semaphore_wait(barrier, bins)
 
     def send_step(s):
-        pack(s + 1, packed, packed_lab)
+        if not (isinstance(s, int) and s == 0):
+            pack(s + 1, packed, packed_lab)
         label_copy(s + 1).start()
         sized(facing(s + 1), lambda size: data_copy(s + 1, size).start())
 
@@ -203,19 +207,19 @@
         forward_label_copy(place).wait_recv()
         sized(chip, lambda size: forward_copy(place, size).wait_recv())
 
-    def tile(side, lab, left, right):
-        left_rows = side[pl.ds(2 * left, 2), :cap, :].reshape(2 * cap, width)
-        left_lab = jnp.concatenate(
-            [lab[2 * left + half].T[:cap, 0:1] for half in range(2)], axis=0)
-        right_rows = own[pl.ds(2 * right, 2)].reshape(2 * LANES, width)
-        right_lab = jnp.concatenate(
-            [own_lab[2 * right + half, 0:1, :] for half in range(2)], axis=1)
+    def tile(side, lab, left, count, pair, half=None):
+        blocks = (0, 1) if half is None else (half,)
+        part = slice(blocks[0] * LANES, (blocks[-1] + 1) * LANES)
+        left_rows = side[pl.ds(left, count), :cap, :].reshape(count * cap, width)
+        left_lab = jnp.concatenate([lab[left + k].T[:cap, 0:1] for k in range(count)], axis=0)
+        right_rows = own[pl.ds(2 * pair + blocks[0], len(blocks))].reshape(-1, width)
+        right_lab = jnp.concatenate([own_lab[2 * pair + k, 0:1, :] for k in blocks], axis=1)
         cosine = lax.dot_general(left_rows, right_rows, NT, preferred_element_type=F32)
         same = left_lab == right_lab
         dens = jnp.where(same, jnp.exp(cosine * (1.0 / SOFTMAX_TEMP)), 0.0)
         cent = jnp.where(same, cosine, 0.0)
-        acc_dens[right] += jnp.sum(dens.reshape(2 * cap // 8, 8, 2 * LANES), axis=0)
-        acc_cent[right] += jnp.sum(cent.reshape(2 * cap // 8, 8, 2 * LANES), axis=0)
+        acc_dens[pair, :, part] += jnp.sum(dens.reshape(count * cap // 8, 8, -1), axis=0)
+        acc_cent[pair, :, part] += jnp.sum(cent.reshape(count * cap // 8, 8, -1), axis=0)
 
     def close(pair):
         dens = jnp.sum(acc_dens[pair], axis=0, keepdims=True)
@@ -232,45 +236,66 @@
             lax.fori_loop(0, count, lambda step, carry: (body(step), carry)[1], 0)
 
     def group(pair):
-        span(pair, lambda q: tile(own, own_lab, pair, q))
-        span(pair, lambda q: tile(own, own_lab, q, pair))
-        tile(own, own_lab, pair, pair)
-        span(pair, lambda q: tile(other, other_lab, q, pair))
+        span(pair, lambda q: tile(own, own_lab, 2 * pair, 2, q))
+        span(pair, lambda q: tile(own, own_lab, 2 * q, 2, pair))
+        tile(own, own_lab, 2 * pair, 2, pair)
+        span(pair, lambda q: tile(other, other_lab, 2 * q, 2, pair))
         arrived(2 * pair)
         arrived(2 * pair + 1)
-
-    def finish_group(pair):
-        span(pair, lambda q: tile(other, other_lab, pair, q))
-        tile(other, other_lab, pair, pair)
+        span(pair, lambda q: tile(other, other_lab, 2 * pair, 2, q))
+        tile(other, other_lab, 2 * pair, 2, pair)
 
     pairs = bins // 2
     take(1)
     group(0)
-    finish_group(0)
 
     def middle(s):
         take(2 * s + 2)
         take(2 * s + 3)
         group(s + 1)
-        finish_group(s + 1)
 
     loop(pairs - 2, middle)
     last = pairs - 1
-    take(2 * last)
-    take(2 * last + 1)
-    group(last)
-    tile(other, other_lab, last, 0)
+    next_last, very_last = 2 * last, 2 * last + 1
+    take(next_last)
+    span(last, lambda q: tile(own, own_lab, next_last, 1, q))
+    span(last, lambda q: tile(own, own_lab, 2 * q, 2, last, 0))
+    tile(own, own_lab, next_last, 1, last, 0)
+    span(last, lambda q: tile(other, other_lab, 2 * q, 2, last, 0))
+    arrived(next_last)
+    span(last, lambda q: tile(other, other_lab, next_last, 1, q))
+    tile(other, other_lab, next_last, 1, last, 0)
+    take(very_last)
+    span(last, lambda q: tile(own, own_lab, very_last, 1, q))
+    tile(own, own_lab, very_last, 1, last, 0)
+    span(pairs, lambda q: tile(own, own_lab, 2 * q, 2, last, 1))
+    span(last, lambda q: tile(other, other_lab, 2 * q, 2, last, 1))
+    tile(other, other_lab, next_last, 1, last, 1)
+    arrived(very_last)
+    tile(other, other_lab, very_last, 1, 0)
     close(0)
     ret_in[0] = ret[0]
     return_copy(1).start()
 
     def answer(s):
-        tile(other, other_lab, last, s + 1)
+        tile(other, other_lab, very_last, 1, s + 1)
         close(s + 1)
         return_copy(2 * s + 2).start()
         return_copy(2 * s + 3).start()
 
     loop(pairs - 1, answer)
+
+    def finish(s):
+        sized(facing(s + 1), lambda size: data_copy(s + 1, size).wait_send())
+        label_copy(s + 1).wait_send()
+
+    loop(bins - 1, finish)
+
+    def finish_forward(s):
+        sized(chip, lambda size: forward_copy(s, size).wait_send())
+        forward_label_copy(s).wait_send()
+
+    loop(bins, finish_forward)
 
     def gathered(place, total):
         values = ret_in[place].T
@@ -294,18 +319,7 @@
     cent = jnp.sum(total[1], axis=0, keepdims=True) / size_row
     out_ref[...] = jnp.concatenate([jnp.log(dens), cent, jnp.zeros((6, rows), F32)], axis=0)
 
-    def finish(s):
-        sized(facing(s + 1), lambda size: data_copy(s + 1, size).wait_send())
-        label_copy(s + 1).wait_send()
-        return_copy(s + 1).wait_send()
-
-    loop(bins - 1, finish)
-
-    def finish_forward(s):
-        sized(chip, lambda size: forward_copy(s, size).wait_send())
-        forward_label_copy(s).wait_send()
-
-    loop(bins, finish_forward)
+    loop(bins - 1, lambda s: return_copy(s + 1).wait_send())
 
 
 def on_device(embeddings, cluster_ids, cluster_sizes):
@@ -343,6 +357,7 @@
             pltpu.VMEM((8, rows), jnp.int32),
             pltpu.VMEM((bins // 2, 8, 2 * LANES), F32),
             pltpu.VMEM((bins // 2, 8, 2 * LANES), F32),
+            pltpu.VMEM((rows, rows), BF16),
             pltpu.SemaphoreType.DMA,
             pltpu.SemaphoreType.DMA,
             pltpu.SemaphoreType.DMA,

time: 32.9 us -> 33.2 us (level)
  Pallas kernels: 30.6 us -> 31 us
    pallas_call x1, Pallas kernels: 30.6 us -> 31 us  [on_device(): pl.pallas_call(functools.partial(kernel, n, cap, tuple(caps), tuple(chips...]
where the time goes in v6:
time: 33.2 us; the launch traced here: 33 us
  Pallas kernels  31 us (93%)
  local copies, waits for them, and re-layouts  1.38 us (4%)
  between operations  0.64 us (2%)
    pallas_call x1, Pallas kernels, on_device(): pl.pallas_call(functools.partial(kernel, n, cap, tuple(caps), tuple(chips...  31 us
    slice x1, local copies, waits for them, and re-layouts, on_device(): return (out[0], out[1])  1.38 us

profile of v6, /device:TPU:0, one launch (start us, length us, event | category | flops | bytes accessed | tf_op | source)
XLA Modules:
  0.0 33.0 jit_solution(11662511798930019734)
XLA Ops:
  0.6 31.0 %shard_map.50 = f32[8,384]{1,0:T(8,128)} custom-call(bf16[384,512]{1,0:T(8,128)(2,1)} %emb_hbm.1, s32[384]{0:T(512)} %ids_hbm.1, s32[64]{0:T(128)} %sizes_hbm.1), custom_call_target="tpu_custom_call" | custom-call | flops 4000000000 | bytes 1000000 | tf_op jit(solution)/shard_map/pallas_call | solution.py:340
  31.6 1.4 %slice_reduce_fusion = (f32[384]{0:T(512)}, f32[384]{0:T(512)}) fusion(f32[8,384]{1,0:T(8,128)} %shard_map.50), kind=kLoop, calls=%fused_computation | loop fusion | bytes 6144 | tf_op jit(solution)/shard_map/slice | solution.py:369

commit v7 on v5

--- a/solution.py
+++ b/solution.py
@@ -10,6 +10,7 @@
 SOFTMAX_TEMP = 0.1
 EPSILON = 1e-06
 LANES = 128
+IN_FLIGHT = 3
 MESH = pl.DeviceIdType.MESH
 F32 = jnp.float32
 BF16 = jnp.bfloat16
@@ -161,15 +162,18 @@
 
     pl.semaphore_wait(barrier, bins)
 
-    def send_step(s):
-        pack(s + 1, packed, packed_lab)
-        label_copy(s + 1).start()
-        sized(facing(s + 1), lambda size: data_copy(s + 1, size).start())
-
-    loop(bins - 1, send_step)
+    def start_send(place):
+        label_copy(place).start()
+        sized(facing(place), lambda size: data_copy(place, size).start())
+
+    ahead_by = min(IN_FLIGHT, bins - 1)
+    for place in range(1, ahead_by + 1):
+        pack(place, packed, packed_lab)
+        start_send(place)
     pack(0, own, own_lab)
     forward_label_copy(0).start()
     sized(chip, lambda size: forward_copy(0, size).start())
+    loop(bins - 1 - ahead_by, lambda s: pack(s + 1 + ahead_by, packed, packed_lab))
 
     def clear(size):
         def step(s):
@@ -198,6 +202,10 @@
             forward_copy(place, size).start()
 
         sized(chip, go)
+        if not isinstance(place, int):
+            pl.when(place + ahead_by < bins)(lambda: start_send(place + ahead_by))
+        elif place + ahead_by < bins:
+            start_send(place + ahead_by)
 
     def arrived(place):
         forward_label_copy(place).wait_recv()
@@ -348,9 +356,9 @@
             pltpu.SemaphoreType.DMA,
         ] + [dma] * 10,
         compiler_params=pltpu.CompilerParams(
-            collective_id=0, has_side_effects=True, vmem_limit_bytes=64 * 1024 * 1024 - 128 * 1024),
+            collective_id=0, has_side_effects=True, vmem_limit_bytes=48 * 1024 * 1024),
         cost_estimate=pl.CostEstimate(flops=4 * 10 ** 9, bytes_accessed=10 ** 6, transcendentals=0),
-    )(embeddings, cluster_ids, cluster_sizes)
+    )(*[pltpu.with_memory_space_constraint(x, pltpu.HBM) for x in (embeddings, cluster_ids, cluster_sizes)])
     return out[0], out[1]
 
 

time: 32.9 us -> 33.1 us (level)
  Pallas kernels: 30.6 us -> 31.7 us
  local copies, waits for them, and re-layouts: 1.38 us -> 0.6 us
    pallas_call x1, Pallas kernels: 30.6 us -> 31.7 us  [on_device(): pl.pallas_call(functools.partial(kernel, n, cap, tuple(caps), tuple(chips...]
    slice x1, local copies, waits for them, and re-layouts: 1.38 us -> 0.6 us  [on_device(): return (out[0], out[1])]
where the time goes in v7:
time: 33.1 us; the launch traced here: 33 us
  Pallas kernels  31.7 us (96%)
  between operations  0.64 us (2%)
  local copies, waits for them, and re-layouts  0.6 us (2%)
    pallas_call x1, Pallas kernels, on_device(): pl.pallas_call(functools.partial(kernel, n, cap, tuple(caps), tuple(chips...  31.7 us

profile of v7, /device:TPU:0, one launch (start us, length us, event | category | flops | bytes accessed | tf_op | source)
XLA Modules:
  0.0 33.0 jit_solution(2157382726834201029)
XLA Ops:
  0.6 31.7 %shard_map.50 = f32[8,384]{1,0:T(8,128)S(1)} custom-call(bf16[384,512]{1,0:T(8,128)(2,1)} %emb_hbm.1, s32[384]{0:T(512)} %ids_hbm.1, s32[64]{0:T(128)} %sizes_hbm.1), custom_call_target="tpu_custom_call" | custom-call | flops 4000000000 | bytes 1000000 | tf_op jit(solution)/shard_map/pallas_call | solution.py:334
  32.4 0.6 %slice_reduce_fusion = (f32[384]{0:T(512)}, f32[384]{0:T(512)}) fusion(f32[8,384]{1,0:T(8,128)S(1)} %shard_map.50), kind=kLoop, calls=%fused_computation | loop fusion | bytes 6144 | tf_op jit(solution)/shard_map/slice | solution.py:362

commit v8 on v5

--- a/solution.py
+++ b/solution.py
@@ -348,9 +348,9 @@
             pltpu.SemaphoreType.DMA,
         ] + [dma] * 10,
         compiler_params=pltpu.CompilerParams(
-            collective_id=0, has_side_effects=True, vmem_limit_bytes=64 * 1024 * 1024 - 128 * 1024),
+            collective_id=0, has_side_effects=True, vmem_limit_bytes=48 * 1024 * 1024),
         cost_estimate=pl.CostEstimate(flops=4 * 10 ** 9, bytes_accessed=10 ** 6, transcendentals=0),
-    )(embeddings, cluster_ids, cluster_sizes)
+    )(*[pltpu.with_memory_space_constraint(x, pltpu.HBM) for x in (embeddings, cluster_ids, cluster_sizes)])
     return out[0], out[1]
 
 

time: 32.9 us -> 31.4 us (0.954)
  local copies, waits for them, and re-layouts: 1.38 us -> 0.6 us
  Pallas kernels: 30.6 us -> 30 us
    slice x1, local copies, waits for them, and re-layouts: 1.38 us -> 0.6 us  [on_device(): return (out[0], out[1])]
    pallas_call x1, Pallas kernels: 30.6 us -> 30 us  [on_device(): pl.pallas_call(functools.partial(kernel, n, cap, tuple(caps), tuple(chips...]
where the time goes in v8:
time: 31.4 us; the launch traced here: 31.3 us
  Pallas kernels  30 us (96%)
  between operations  0.64 us (2%)
  local copies, waits for them, and re-layouts  0.6 us (2%)
    pallas_call x1, Pallas kernels, on_device(): pl.pallas_call(functools.partial(kernel, n, cap, tuple(caps), tuple(chips...  30 us

profile of v8, /device:TPU:0, one launch (start us, length us, event | category | flops | bytes accessed | tf_op | source)
XLA Modules:
  0.0 31.3 jit_solution(5627088865174216169)
XLA Ops:
  0.6 30.0 %shard_map.50 = f32[8,384]{1,0:T(8,128)S(1)} custom-call(bf16[384,512]{1,0:T(8,128)(2,1)} %emb_hbm.1, s32[384]{0:T(512)} %ids_hbm.1, s32[64]{0:T(128)} %sizes_hbm.1), custom_call_target="tpu_custom_call" | custom-call | flops 4000000000 | bytes 1000000 | tf_op jit(solution)/shard_map/pallas_call | solution.py:326
  30.7 0.6 %slice_reduce_fusion = (f32[384]{0:T(512)}, f32[384]{0:T(512)}) fusion(f32[8,384]{1,0:T(8,128)S(1)} %shard_map.50), kind=kLoop, calls=%fused_computation | loop fusion | bytes 6144 | tf_op jit(solution)/shard_map/slice | solution.py:354
